TPU v7x, 512 devices: a whole 4x8x8 slice. The times are simulated.
512 devices in a mesh: ctx: 64 (over x, z, core), ch: 8 (over y).
Axes of the slice: x: 4, y: 8, z: 8, core: 2. Of those that a mesh axis runs over, the one named last changes fastest.
Arguments:
- q_in: bfloat16 [8192, 4096], P('ctx', 'ch'), may hold values from -6 to 6
- k_in: bfloat16 [8192, 4096], P('ctx', 'ch'), may hold values from -6 to 6
- v_in: bfloat16 [8192, 4096], P('ctx', 'ch'), may hold values from -6 to 6
- grad_out: bfloat16 [8192, 4096], P('ctx', 'ch'), may hold values from -30 to 30
- short_filter: float32 [3, 4096], P(None, 'ch'), may hold values from -3 to 3
- kernel: float32 [8192, 4096], P('ctx', 'ch'), may hold values from -0.0625 to 0.0625
- skip: float32 [4096], P('ch'), may hold values from -3 to 3
Outputs:
- mixed: bfloat16 [8192, 4096], P('ctx', 'ch')
- grad_q: bfloat16 [8192, 4096], P('ctx', 'ch')
- grad_k: bfloat16 [8192, 4096], P('ctx', 'ch')
- grad_v: bfloat16 [8192, 4096], P('ctx', 'ch')
- grad_short: float32 [3, 4096], P(None, 'ch')
- grad_skip: float32 [4096], P('ch')
- grad_kernel: float32 [8192, 4096], P('ctx', 'ch')
All inputs are finite; a program needn't handle non-finite values.
Results may differ from a plain program's by a relative error of at most 0.009.
Values may be sent and summed in bfloat16 or wider, within the bound.
A program may use at most 64 MiB of HBM per device.

v0:
```python
import math
import jax
import jax.numpy as jnp
from jax import lax
from jax.sharding import PartitionSpec as P

highest = lax.Precision.HIGHEST


def shifted(shard, axis, by):
    size = lax.axis_size(axis)
    pairs = [(i, i + by) for i in range(size) if 0 <= i + by < size]
    return lax.ppermute(shard, axis, pairs)


def phase(left_idx, right_idx, period):
    product = left_idx[:, None] * right_idx[None, :] % period
    return product.astype(jnp.float32) * (2.0 * math.pi / period)


def forward_table(angle):
    cosine = jnp.cos(angle)
    sine = jnp.sin(angle)
    return jnp.stack([jnp.stack([cosine, sine]), jnp.stack([-sine, cosine])])


def inverse_table(angle):
    cosine = jnp.cos(angle)
    sine = jnp.sin(angle)
    return jnp.stack([jnp.stack([cosine, -sine]), jnp.stack([sine, cosine])])


def short_forward(extended, short_taps, rows_here):
    halo_rows = short_taps.shape[0] - 1
    result = short_taps[0] * extended[halo_rows : halo_rows + rows_here]
    for shift_idx in range(1, short_taps.shape[0]):
        result = (
            result
            + short_taps[shift_idx]
            * extended[halo_rows - shift_idx : halo_rows - shift_idx + rows_here]
        )
    return result


def short_backward(extended, short_taps, rows_here):
    result = short_taps[0] * extended[0:rows_here]
    for shift_idx in range(1, short_taps.shape[0]):
        result = result + short_taps[shift_idx] * extended[shift_idx : shift_idx + rows_here]
    return result


def spread_rows(signal, pieces):
    return lax.all_to_all(
        signal.reshape(pieces, signal.shape[0] // pieces, signal.shape[1]),
        "ctx",
        split_axis=0,
        concat_axis=0,
        tiled=True,
    )


def spectrum_tiles(section_in, here_idx, pieces):
    signals, _, slice_rows, channels = section_in.shape
    rows_here = pieces * slice_rows
    fft_len = 2 * pieces * rows_here
    outer_angle = phase(jnp.arange(2 * pieces), jnp.arange(pieces), 2 * pieces)
    outer_table = jnp.stack([jnp.cos(outer_angle), -jnp.sin(outer_angle)])
    part = jnp.einsum("pba,garc->pgbrc", outer_table, section_in, precision=highest)
    part_re = part[0]
    part_im = part[1]
    twist_angle = phase(
        jnp.arange(2 * pieces), here_idx * slice_rows + jnp.arange(slice_rows), fft_len
    )
    twist_cos = jnp.cos(twist_angle)[None, :, :, None]
    twist_sin = jnp.sin(twist_angle)[None, :, :, None]
    turn_re = part_re * twist_cos + part_im * twist_sin
    turn_im = part_im * twist_cos - part_re * twist_sin
    stacked = jnp.stack([turn_re, turn_im]).reshape(2, signals, pieces, 2, slice_rows, channels)
    arrived = lax.all_to_all(stacked, "ctx", split_axis=2, concat_axis=4, tiled=True).reshape(
        2, signals, 2, rows_here, channels
    )
    inner_angle = phase(jnp.arange(rows_here), jnp.arange(rows_here), rows_here)
    spec = jnp.einsum("pqer,qgjrc->pgjec", forward_table(inner_angle), arrived, precision=highest)
    return (spec[0], spec[1])


def rows_from_spectrum(spec_re, spec_im, here_idx, pieces):
    signals, _, rows_here, channels = spec_re.shape
    slice_rows = rows_here // pieces
    fft_len = 2 * pieces * rows_here
    inner_angle = phase(jnp.arange(rows_here), jnp.arange(rows_here), rows_here)
    part = jnp.einsum(
        "pqre,qgjec->pgjrc",
        inverse_table(inner_angle),
        jnp.stack([spec_re, spec_im]),
        precision=highest,
    )
    part_re = part[0]
    part_im = part[1]
    twist_angle = phase(2 * here_idx + jnp.arange(2), jnp.arange(rows_here), fft_len)
    twist_cos = jnp.cos(twist_angle)[None, :, :, None]
    twist_sin = jnp.sin(twist_angle)[None, :, :, None]
    turn_re = part_re * twist_cos - part_im * twist_sin
    turn_im = part_im * twist_cos + part_re * twist_sin
    stacked = jnp.stack([turn_re, turn_im]).reshape(2, signals, 2, pieces, slice_rows, channels)
    arrived = lax.all_to_all(stacked, "ctx", split_axis=3, concat_axis=2, tiled=True).reshape(
        2, signals, 2 * pieces, slice_rows, channels
    )
    outer_angle = phase(jnp.arange(pieces), jnp.arange(2 * pieces), 2 * pieces)
    outer_table = jnp.stack([jnp.cos(outer_angle), -jnp.sin(outer_angle)])
    time_rows = jnp.einsum("qab,qgbrc->garc", outer_table, arrived, precision=highest) / fft_len
    returned = lax.all_to_all(time_rows, "ctx", split_axis=1, concat_axis=1, tiled=True)
    return returned.reshape(signals, rows_here, channels)


def body(q_in, k_in, v_in, grad_out, short_filter, kernel, skip):
    pieces = lax.axis_size("ctx")
    here_idx = lax.axis_index("ctx")
    rows_here, channels = q_in.shape
    seq_len = pieces * rows_here
    halo_rows = short_filter.shape[0] - 1
    lead = shifted(
        (
            q_in[rows_here - halo_rows :],
            k_in[rows_here - halo_rows :],
            v_in[rows_here - halo_rows :],
        ),
        "ctx",
        1,
    )
    q_ext = jnp.concatenate([lead[0], q_in], axis=0).astype(jnp.float32)
    k_ext = jnp.concatenate([lead[1], k_in], axis=0).astype(jnp.float32)
    v_ext = jnp.concatenate([lead[2], v_in], axis=0).astype(jnp.float32)
    q_short = short_forward(q_ext, short_filter, rows_here)
    k_short = short_forward(k_ext, short_filter, rows_here)
    v_short = short_forward(v_ext, short_filter, rows_here)
    product = (k_short * v_short).astype(jnp.bfloat16)
    product_wide = product.astype(jnp.float32)
    slice_rows = rows_here // pieces
    kernel_tiles = lax.all_to_all(
        kernel.reshape(pieces, slice_rows, channels), "ctx", split_axis=0, concat_axis=0, tiled=True
    )
    product_tiles = spread_rows(product, pieces).astype(jnp.float32)
    spec_re, spec_im = spectrum_tiles(jnp.stack([product_tiles, kernel_tiles]), here_idx, pieces)
    signal_re = spec_re[0]
    signal_im = spec_im[0]
    kernel_re = spec_re[1]
    kernel_im = spec_im[1]
    conv_re = signal_re * kernel_re - signal_im * kernel_im
    conv_im = signal_re * kernel_im + signal_im * kernel_re
    conv = rows_from_spectrum(conv_re[None], conv_im[None], here_idx, pieces)[0]
    filtered = conv + skip[None, :] * product_wide
    mixed = (q_short * filtered).astype(jnp.bfloat16)
    upstream = grad_out.astype(jnp.float32)
    back_q = upstream * filtered
    back_mix = upstream * q_short
    back_cast = back_mix.astype(jnp.bfloat16)
    cotan_tiles = spread_rows(back_cast, pieces).astype(jnp.float32)
    cotan_re, cotan_im = spectrum_tiles(cotan_tiles[None], here_idx, pieces)
    grad_re = cotan_re[0]
    grad_im = cotan_im[0]
    corr_re = kernel_re * grad_re + kernel_im * grad_im
    corr_im = kernel_re * grad_im - kernel_im * grad_re
    lag_re = signal_re * grad_re + signal_im * grad_im
    lag_im = signal_re * grad_im - signal_im * grad_re
    returned = rows_from_spectrum(
        jnp.stack([corr_re, lag_re]), jnp.stack([corr_im, lag_im]), here_idx, pieces
    )
    correlate = returned[0]
    kernel_grad = returned[1]
    back_prod = correlate + skip[None, :] * back_mix
    back_k = back_prod * v_short
    back_v = back_prod * k_short
    tail = shifted((back_q[:halo_rows], back_k[:halo_rows], back_v[:halo_rows]), "ctx", -1)
    grad_q = short_backward(
        jnp.concatenate([back_q, tail[0]], axis=0), short_filter, rows_here
    ).astype(jnp.bfloat16)
    grad_k = short_backward(
        jnp.concatenate([back_k, tail[1]], axis=0), short_filter, rows_here
    ).astype(jnp.bfloat16)
    grad_v = short_backward(
        jnp.concatenate([back_v, tail[2]], axis=0), short_filter, rows_here
    ).astype(jnp.bfloat16)
    tap_rows = []
    for shift_idx in range(short_filter.shape[0]):
        first = halo_rows - shift_idx
        tap_rows.append(
            jnp.sum(
                back_q * q_ext[first : first + rows_here]
                + back_k * k_ext[first : first + rows_here]
                + back_v * v_ext[first : first + rows_here],
                axis=0,
            )
        )
    short_grad = jnp.stack(tap_rows)
    skip_grad = jnp.sum(back_mix * product_wide, axis=0)
    kernel_square = jnp.sum(kernel_grad * kernel_grad)
    summed = lax.psum((short_grad, skip_grad, kernel_square), "ctx")
    local_square = jnp.sum(summed[0] * summed[0]) + jnp.sum(summed[1] * summed[1]) + summed[2]
    norm_sq = lax.psum(local_square, "ch")
    clip_limit = math.sqrt(float(seq_len * channels * lax.axis_size("ch")))
    factor = clip_limit / jnp.maximum(jnp.sqrt(norm_sq), clip_limit)
    return (
        mixed,
        grad_q,
        grad_k,
        grad_v,
        factor * summed[0],
        factor * summed[1],
        factor * kernel_grad,
    )


def solution(mesh):
    in_specs = (
        P("ctx", "ch"),
        P("ctx", "ch"),
        P("ctx", "ch"),
        P("ctx", "ch"),
        P(None, "ch"),
        P("ctx", "ch"),
        P("ch"),
    )
    out_specs = (
        P("ctx", "ch"),
        P("ctx", "ch"),
        P("ctx", "ch"),
        P("ctx", "ch"),
        P(None, "ch"),
        P("ch"),
        P("ctx", "ch"),
    )
    return jax.shard_map(body, mesh=mesh, in_specs=in_specs, out_specs=out_specs, check_vma=False)
```

profile of v0, /device:TPU:1, one launch (start us, length us, event | category | flops | bytes accessed | tf_op | source)
XLA Modules:
  0.0 605.5 jit_solution(6001677519297526203)
XLA Ops:
  1.3 5.4 collective-permute-start.2
  10.1 4.4 collective-permute-start
  20.9 13.8 %all-to-all-start = ((bf16[64,2,512]{2,1,0:T(2,128)(2,1)}), bf16[64,2,512]{2,1,0:T(2,128)(2,1)S(1)}, u32[]{:S(2)}, u32[]{:S(2)}) async-start(bf16[64,2,512]{2,1,0:T(2,128)(2,1)} %reshape.558), calls=%async_computation | async-start | bytes 262144 | tf_op jit(solution)/shard_map/all_to_all | solution.py:53
  35.6 9.4 %all-to-all-done = bf16[64,2,512]{2,1,0:T(2,128)(2,1)S(1)} async-done(((bf16[64,2,512]{2,1,0:T(2,128)(2,1)}), bf16[64,2,512]{2,1,0:T(2,128)(2,1)S(1)}, u32[]{:S(2)}, u32[]{:S(2)}) %all-to-all-start) | async-done | bytes 131104 | tf_op jit(solution)/shard_map/all_to_all | solution.py:53
  45.0 4.9 all-to-all-start.5
  50.9 9.4 %all-to-all-done.5 = bf16[64,2,512]{2,1,0:T(2,128)(2,1)S(1)} async-done(((bf16[64,2,512]{2,1,0:T(2,128)(2,1)}), bf16[64,2,512]{2,1,0:T(2,128)(2,1)S(1)}, u32[]{:S(2)}, u32[]{:S(2)}) %all-to-all-start.5) | async-done | bytes 131104 | tf_op jit(solution)/shard_map/all_to_all | solution.py:53
  60.3 4.9 all-to-all-start.1
  68.8 8.4 %all-to-all-done.1 = f32[64,2,512]{2,1,0:T(2,128)S(1)} async-done(((f32[64,2,512]{2,1,0:T(2,128)}), f32[64,2,512]{2,1,0:T(2,128)S(1)}, u32[]{:S(2)}, u32[]{:S(2)}) %all-to-all-start.1) | async-done | bytes 262176 | tf_op jit(solution)/shard_map/all_to_all | solution.py:140
  77.2 6.4 %all-to-all-start.6 = ((f32[2,1,64,2,2,512]{5,3,4,0,1,2:T(2,128)}), f32[2,1,64,2,2,512]{5,3,4,0,1,2:T(2,128)S(1)}, u32[]{:S(2)}, u32[]{:S(2)}) async-start(f32[2,1,64,2,2,512]{5,3,4,0,1,2:T(2,128)} %copy.108), calls=%async_computation.6 | async-start | bytes 2097152 | tf_op jit(solution)/shard_map/all_to_all | solution.py:79
  96.5 15.5 %all-to-all-done.6 = f32[2,1,64,2,2,512]{5,3,4,0,1,2:T(2,128)S(1)} async-done(((f32[2,1,64,2,2,512]{5,3,4,0,1,2:T(2,128)}), f32[2,1,64,2,2,512]{5,3,4,0,1,2:T(2,128)S(1)}, u32[]{:S(2)}, u32[]{:S(2)}) %all-to-all-start.6) | async-done | bytes 1048608 | tf_op jit(solution)/shard_map/all_to_all | solution.py:79
  113.0 6.8 %all-to-all-start.2 = ((f32[2,2,64,2,2,512]{5,3,4,1,0,2:T(2,128)}), f32[2,2,64,2,2,512]{5,3,4,1,0,2:T(2,128)S(1)}, u32[]{:S(2)}, u32[]{:S(2)}) async-start(f32[2,2,64,2,2,512]{5,3,4,1,0,2:T(2,128)} %copy.100), calls=%async_computation.2 | async-start | bytes 4194304 | tf_op jit(solution)/shard_map/all_to_all | solution.py:79
  129.4 41.6 %all-to-all-done.2 = f32[2,2,64,2,2,512]{5,3,4,1,0,2:T(2,128)S(1)} async-done(((f32[2,2,64,2,2,512]{5,3,4,1,0,2:T(2,128)}), f32[2,2,64,2,2,512]{5,3,4,1,0,2:T(2,128)S(1)}, u32[]{:S(2)}, u32[]{:S(2)}) %all-to-all-start.2) | async-done | bytes 2097184 | tf_op jit(solution)/shard_map/all_to_all | solution.py:79
  172.0 3.4 fusion.4
  187.9 6.3 %all-to-all-start.3 = ((f32[2,1,2,64,2,512]{5,4,2,1,0,3:T(2,128)}), f32[2,1,2,64,2,512]{5,4,2,1,0,3:T(2,128)}, u32[]{:S(2)}, u32[]{:S(2)}) async-start(f32[2,1,2,64,2,512]{5,4,2,1,0,3:T(2,128)} %copy.105), calls=%async_computation.3 | async-start | bytes 2097152 | tf_op jit(solution)/shard_map/all_to_all | solution.py:106
  206.3 16.1 %all-to-all-done.3 = f32[2,1,2,64,2,512]{5,4,2,1,0,3:T(2,128)} async-done(((f32[2,1,2,64,2,512]{5,4,2,1,0,3:T(2,128)}), f32[2,1,2,64,2,512]{5,4,2,1,0,3:T(2,128)}, u32[]{:S(2)}, u32[]{:S(2)}) %all-to-all-start.3) | async-done | bytes 1048608 | tf_op jit(solution)/shard_map/all_to_all | solution.py:106
  222.5 6.2 %all-to-all-start.7 = ((f32[2,2,2,64,2,512]{5,4,2,1,0,3:T(2,128)}), f32[2,2,2,64,2,512]{5,4,2,1,0,3:T(2,128)S(1)}, u32[]{:S(2)}, u32[]{:S(2)}) async-start(f32[2,2,2,64,2,512]{5,4,2,1,0,3:T(2,128)} %copy.112), calls=%async_computation.7 | async-start | bytes 4194304 | tf_op jit(solution)/shard_map/all_to_all | solution.py:106
  237.4 42.5 %all-to-all-done.7 = f32[2,2,2,64,2,512]{5,4,2,1,0,3:T(2,128)S(1)} async-done(((f32[2,2,2,64,2,512]{5,4,2,1,0,3:T(2,128)}), f32[2,2,2,64,2,512]{5,4,2,1,0,3:T(2,128)S(1)}, u32[]{:S(2)}, u32[]{:S(2)}) %all-to-all-start.7) | async-done | bytes 2097184 | tf_op jit(solution)/shard_map/all_to_all | solution.py:106
  279.9 6.1 %all-to-all-start.4 = ((f32[1,64,2,512]{3,2,0,1:T(2,128)}), f32[1,64,2,512]{3,2,0,1:T(2,128)S(1)}, u32[]{:S(2)}, u32[]{:S(2)}) async-start(f32[1,64,2,512]{3,2,0,1:T(2,128)} %copy.69), calls=%async_computation.4 | async-start | bytes 524288 | tf_op jit(solution)/shard_map/all_to_all | solution.py:112
  293.9 4.0 all-to-all-done.4
  297.9 6.3 %all-to-all-start.8 = ((f32[2,64,2,512]{3,2,0,1:T(2,128)}), f32[2,64,2,512]{3,2,0,1:T(2,128)S(1)}, u32[]{:S(2)}, u32[]{:S(2)}) async-start(f32[2,64,2,512]{3,2,0,1:T(2,128)} %copy.83), calls=%async_computation.8 | async-start | bytes 1048576 | tf_op jit(solution)/shard_map/all_to_all | solution.py:112
  304.5 17.1 %all-to-all-done.8 = f32[2,64,2,512]{3,2,0,1:T(2,128)S(1)} async-done(((f32[2,64,2,512]{3,2,0,1:T(2,128)}), f32[2,64,2,512]{3,2,0,1:T(2,128)S(1)}, u32[]{:S(2)}, u32[]{:S(2)}) %all-to-all-start.8) | async-done | bytes 524320 | tf_op jit(solution)/shard_map/all_to_all | solution.py:112
  324.7 242.6 %all-reduce = (f32[3,512]{1,0:T(4,128)S(1)}, f32[512]{0:T(512)S(1)}, f32[]{:T(128)}) all-reduce(f32[3,512]{1,0:T(4,128)S(1)} %pad_maximum_fusion.23, f32[512]{0:T(512)S(1)} %get-tuple-element.13, f32[]{:T(128)} %get-tuple-element.34), channel_id=1, replica_groups=mesh['ctx'=64,'ch'=8] {'ctx'}, use_global_device_ids=true, to_apply=%region_3.4 | all-reduce | flops 2049 | bytes 16392 | tf_op jit(solution)/shard_map/psum | solution.py:198
  570.5 14.4 %psum.31 = f32[]{:T(128)} all-reduce(f32[]{:T(128)S(6)} %add.288), channel_id=1, replica_groups=mesh['ctx'=64,'ch'=8] {'ch'}, use_global_device_ids=true, to_apply=%region_10.11 | all-reduce | flops 1 | bytes 8 | tf_op jit(solution)/shard_map/psum | solution.py:200
  586.2 11.3 %collective-permute-start.3 = (f32[2,512]{1,0:T(2,128)S(1)}, f32[2,512]{1,0:T(2,128)S(1)}, u32[]{:S(2)}, u32[]{:S(2)}) collective-permute-start(f32[2,512]{1,0:T(2,128)S(1)} %slice.213), channel_id=1, source_target_pairs={{8,0},{16,8},{24,16},{32,24},{40,32},{48,40},{56,48},{64,56},{72,6... | collective-permute-start | bytes 12296 | tf_op jit(solution)/shard_map/ppermute | solution.py:13
  (113 shorter events, 94.1 us)
Async XLA Ops:
  1.3 15.8 %collective-permute-start.2 = (bf16[2,512]{1,0:T(2,128)(2,1)S(1)}, bf16[2,512]{1,0:T(2,128)(2,1)S(1)}, u32[]{:S(2)}, u32[]{:S(2)}) collective-permute-start(bf16[2,512]{1,0:T(2,128)(2,1)S(1)} %slice.167), channel_id=1, source_target_pairs={{0,8},{8,16},{16,24},{24,32},{32,40},{40,48},{48,56},{56,64},{64,7... | collective-permute-start | bytes 6152 | tf_op jit(solution)/shard_map/ppermute | solution.py:13
  7.4 8.8 %collective-permute-start.1 = (bf16[2,512]{1,0:T(2,128)(2,1)S(1)}, bf16[2,512]{1,0:T(2,128)(2,1)S(1)}, u32[]{:S(2)}, u32[]{:S(2)}) collective-permute-start(bf16[2,512]{1,0:T(2,128)(2,1)S(1)} %slice.163), channel_id=1, source_target_pairs={{0,8},{8,16},{16,24},{24,32},{32,40},{40,48},{48,56},{56,64},{64,7... | collective-permute-start | bytes 6152 | tf_op jit(solution)/shard_map/ppermute | solution.py:13
  10.1 5.2 collective-permute-start
  18.1 16.7 %copy-start.9 = (bf16[128,512]{1,0:T(8,128)(2,1)S(1)}, bf16[128,512]{1,0:T(8,128)(2,1)}, u32[]{:S(2)}) copy-start(bf16[128,512]{1,0:T(8,128)(2,1)} %param.10) | copy-start | bytes 393220
  18.1 31.8 %copy-start.11 = (f32[128,512]{1,0:T(8,128)S(1)}, f32[128,512]{1,0:T(8,128)}, u32[]{:S(2)}) copy-start(f32[128,512]{1,0:T(8,128)} %param.12) | copy-start | bytes 786436
  20.2 45.6 %copy-start.7 = (bf16[128,512]{1,0:T(8,128)(2,1)}, bf16[128,512]{1,0:T(8,128)(2,1)S(1)}, u32[]{:S(2)}) copy-start(bf16[128,512]{1,0:T(8,128)(2,1)S(1)} %get-tuple-element.14) | copy-start | bytes 393220
  20.9 24.2 %all-to-all-start = ((bf16[64,2,512]{2,1,0:T(2,128)(2,1)}), bf16[64,2,512]{2,1,0:T(2,128)(2,1)S(1)}, u32[]{:S(2)}, u32[]{:S(2)}) async-start(bf16[64,2,512]{2,1,0:T(2,128)(2,1)} %reshape.558), calls=%async_computation | async-start | bytes 262144 | tf_op jit(solution)/shard_map/all_to_all | solution.py:53
  45.0 15.2 %all-to-all-start.5 = ((bf16[64,2,512]{2,1,0:T(2,128)(2,1)}), bf16[64,2,512]{2,1,0:T(2,128)(2,1)S(1)}, u32[]{:S(2)}, u32[]{:S(2)}) async-start(bf16[64,2,512]{2,1,0:T(2,128)(2,1)} %reshape.563), calls=%async_computation.5 | async-start | bytes 262144 | tf_op jit(solution)/shard_map/all_to_all | solution.py:53
  60.3 16.9 %all-to-all-start.1 = ((f32[64,2,512]{2,1,0:T(2,128)}), f32[64,2,512]{2,1,0:T(2,128)S(1)}, u32[]{:S(2)}, u32[]{:S(2)}) async-start(f32[64,2,512]{2,1,0:T(2,128)} %reshape.559), calls=%async_computation.1 | async-start | bytes 524288 | tf_op jit(solution)/shard_map/all_to_all | solution.py:140
  77.2 34.9 %all-to-all-start.6 = ((f32[2,1,64,2,2,512]{5,3,4,0,1,2:T(2,128)}), f32[2,1,64,2,2,512]{5,3,4,0,1,2:T(2,128)S(1)}, u32[]{:S(2)}, u32[]{:S(2)}) async-start(f32[2,1,64,2,2,512]{5,3,4,0,1,2:T(2,128)} %copy.108), calls=%async_computation.6 | async-start | bytes 2097152 | tf_op jit(solution)/shard_map/all_to_all | solution.py:79
  113.0 58.0 %all-to-all-start.2 = ((f32[2,2,64,2,2,512]{5,3,4,1,0,2:T(2,128)}), f32[2,2,64,2,2,512]{5,3,4,1,0,2:T(2,128)S(1)}, u32[]{:S(2)}, u32[]{:S(2)}) async-start(f32[2,2,64,2,2,512]{5,3,4,1,0,2:T(2,128)} %copy.100), calls=%async_computation.2 | async-start | bytes 4194304 | tf_op jit(solution)/shard_map/all_to_all | solution.py:79
  187.9 34.6 %all-to-all-start.3 = ((f32[2,1,2,64,2,512]{5,4,2,1,0,3:T(2,128)}), f32[2,1,2,64,2,512]{5,4,2,1,0,3:T(2,128)}, u32[]{:S(2)}, u32[]{:S(2)}) async-start(f32[2,1,2,64,2,512]{5,4,2,1,0,3:T(2,128)} %copy.105), calls=%async_computation.3 | async-start | bytes 2097152 | tf_op jit(solution)/shard_map/all_to_all | solution.py:106
  194.2 1.5 copy-start.1
  194.2 1.7 copy-start.4
  200.0 1.6 copy-start.3
  222.5 57.4 %all-to-all-start.7 = ((f32[2,2,2,64,2,512]{5,4,2,1,0,3:T(2,128)}), f32[2,2,2,64,2,512]{5,4,2,1,0,3:T(2,128)S(1)}, u32[]{:S(2)}, u32[]{:S(2)}) async-start(f32[2,2,2,64,2,512]{5,4,2,1,0,3:T(2,128)} %copy.112), calls=%async_computation.7 | async-start | bytes 4194304 | tf_op jit(solution)/shard_map/all_to_all | solution.py:106
  279.9 18.0 %all-to-all-start.4 = ((f32[1,64,2,512]{3,2,0,1:T(2,128)}), f32[1,64,2,512]{3,2,0,1:T(2,128)S(1)}, u32[]{:S(2)}, u32[]{:S(2)}) async-start(f32[1,64,2,512]{3,2,0,1:T(2,128)} %copy.69), calls=%async_computation.4 | async-start | bytes 524288 | tf_op jit(solution)/shard_map/all_to_all | solution.py:112
  292.7 29.9 %copy-start.8 = (bf16[128,512]{1,0:T(8,128)(2,1)S(1)}, bf16[128,512]{1,0:T(8,128)(2,1)}, u32[]{:S(2)}) copy-start(bf16[128,512]{1,0:T(8,128)(2,1)} %copy-done.7) | copy-start | bytes 393220
  292.7 29.9 %copy-start.10 = (bf16[128,512]{1,0:T(8,128)(2,1)S(1)}, bf16[128,512]{1,0:T(8,128)(2,1)}, u32[]{:S(2)}) copy-start(bf16[128,512]{1,0:T(8,128)(2,1)} %param.10) | copy-start | bytes 393220
  292.7 29.9 %copy-start.12 = (f32[512]{0:T(512)S(1)}, f32[512]{0:T(512)}, u32[]{:S(2)}) copy-start(f32[512]{0:T(512)} %param.13) | copy-start | bytes 6148
  297.9 23.6 %all-to-all-start.8 = ((f32[2,64,2,512]{3,2,0,1:T(2,128)}), f32[2,64,2,512]{3,2,0,1:T(2,128)S(1)}, u32[]{:S(2)}, u32[]{:S(2)}) async-start(f32[2,64,2,512]{3,2,0,1:T(2,128)} %copy.83), calls=%async_computation.8 | async-start | bytes 1048576 | tf_op jit(solution)/shard_map/all_to_all | solution.py:112
  586.2 16.7 %collective-permute-start.3 = (f32[2,512]{1,0:T(2,128)S(1)}, f32[2,512]{1,0:T(2,128)S(1)}, u32[]{:S(2)}, u32[]{:S(2)}) collective-permute-start(f32[2,512]{1,0:T(2,128)S(1)} %slice.213), channel_id=1, source_target_pairs={{8,0},{16,8},{24,16},{32,24},{40,32},{48,40},{56,48},{64,56},{72,6... | collective-permute-start | bytes 12296 | tf_op jit(solution)/shard_map/ppermute | solution.py:13
  597.5 5.4 collective-permute-start.4
  599.4 4.9 collective-permute-start.5
  (4 other events, 4.1 us)
where the time goes:
time: 613 us; the launch traced here: 606 us
  blocking collectives  257 us (42%)
  waiting for transfers between devices  166 us (27%)
  starting transfers between devices  88.6 us (14%)
  local copies, waits for them, and re-layouts  48.5 us (8%)
  other arithmetic  25.9 us (4%)
  matrix products  16 us (3%)
    psum x1, blocking collectives, body(): summed = lax.psum((short_grad, skip_grad, kernel_square), 'ctx')  243 us
    all_to_all x2, waiting for transfers between devices, rows_from_spectrum(): lax.all_to_all(stacked, 'ctx', split_axis=3, concat_axis=2, tiled=True)  58.6 us
    all_to_all x2, waiting for transfers between devices, spectrum_tiles(): lax.all_to_all(stacked, 'ctx', split_axis=2, concat_axis=4, tiled=True)  57.1 us
    ppermute x6, starting transfers between devices, shifted(): return lax.ppermute(shard, axis, pairs)  26.8 us
    all_to_all x2, waiting for transfers between devices, rows_from_spectrum(): lax.all_to_all(time_rows, 'ctx', split_axis=1, concat_axis=1, tiled=True)  21.1 us
    all_to_all x2, waiting for transfers between devices, spread_rows(): lax.all_to_all(signal.reshape(pieces, signal.shape[0] // pieces, signal.s...  18.8 us
    all_to_all x2, starting transfers between devices, spread_rows(): lax.all_to_all(signal.reshape(pieces, signal.shape[0] // pieces, signal.s...  18.7 us
    psum x1, blocking collectives, body(): norm_sq = lax.psum(local_square, 'ch')  14.4 us
  transfers between devices with their start and end apart: 15, of which 10 were waited for; matrix products, arithmetic and copies ran while one was open for 10% of the time, Pallas kernels for 0%

commit v1 on v0

--- a/solution.py
+++ b/solution.py
@@ -197,7 +197,9 @@
     kernel_square = jnp.sum(kernel_grad * kernel_grad)
     summed = lax.psum((short_grad, skip_grad, kernel_square), "ctx")
     local_square = jnp.sum(summed[0] * summed[0]) + jnp.sum(summed[1] * summed[1]) + summed[2]
-    norm_sq = lax.psum(local_square, "ch")
+    norm_sq = local_square
+    for hop in (1, 2, 4):
+        norm_sq = norm_sq + lax.ppermute(norm_sq, "ch", [(dev, dev ^ hop) for dev in range(8)])
     clip_limit = math.sqrt(float(seq_len * channels * lax.axis_size("ch")))
     factor = clip_limit / jnp.maximum(jnp.sqrt(norm_sq), clip_limit)
     return (

time: 613 us -> 613 us (level)
  blocking collectives: 257 us -> 243 us
  starting transfers between devices: 88.6 us -> 102 us
    ppermute x0 -> x3, starting transfers between devices: none -> 16.1 us  [body(): lax.ppermute(norm_sq, 'ch', [(dev, dev ^ hop) for dev in range(8)])]
    psum x1 -> x0, blocking collectives: 14.4 us -> none  [body(): norm_sq = lax.psum(local_square, 'ch')]
  transfers between devices with their start and end apart: 15 -> 18, of which waited for: 10 -> 11; matrix products, arithmetic and copies ran while one was open for 10% -> 10% of each run, Pallas kernels for 0% -> 0%
where the time goes in v1:
time: 613 us; the launch traced here: 606 us
  blocking collectives  243 us (40%)
  waiting for transfers between devices  166 us (27%)
  starting transfers between devices  102 us (17%)
  local copies, waits for them, and re-layouts  48.5 us (8%)
  other arithmetic  25.8 us (4%)
  matrix products  16 us (3%)
    psum x1, blocking collectives, body(): summed = lax.psum((short_grad, skip_grad, kernel_square), 'ctx')  243 us
    all_to_all x2, waiting for transfers between devices, rows_from_spectrum(): lax.all_to_all(stacked, 'ctx', split_axis=3, concat_axis=2, tiled=True)  58.6 us
    all_to_all x2, waiting for transfers between devices, spectrum_tiles(): lax.all_to_all(stacked, 'ctx', split_axis=2, concat_axis=4, tiled=True)  57.2 us
    ppermute x6, starting transfers between devices, shifted(): return lax.ppermute(shard, axis, pairs)  23.9 us
    all_to_all x2, waiting for transfers between devices, rows_from_spectrum(): lax.all_to_all(time_rows, 'ctx', split_axis=1, concat_axis=1, tiled=True)  21.1 us
    all_to_all x2, waiting for transfers between devices, spread_rows(): lax.all_to_all(signal.reshape(pieces, signal.shape[0] // pieces, signal.s...  18.8 us
    all_to_all x2, starting transfers between devices, spread_rows(): lax.all_to_all(signal.reshape(pieces, signal.shape[0] // pieces, signal.s...  18.7 us
    ppermute x3, starting transfers between devices, body(): lax.ppermute(norm_sq, 'ch', [(dev, dev ^ hop) for dev in range(8)])  16.1 us
  transfers between devices with their start and end apart: 18, of which 11 were waited for; matrix products, arithmetic and copies ran while one was open for 10% of the time, Pallas kernels for 0%

profile of v1, /device:TPU:1, one launch (start us, length us, event | category | flops | bytes accessed | tf_op | source)
XLA Modules:
  0.0 605.6 jit_solution(1878154955358240050)
XLA Ops:
  1.3 5.4 collective-permute-start.2
  10.1 4.4 collective-permute-start
  20.9 13.8 %all-to-all-start = ((bf16[64,2,512]{2,1,0:T(2,128)(2,1)}), bf16[64,2,512]{2,1,0:T(2,128)(2,1)S(1)}, u32[]{:S(2)}, u32[]{:S(2)}) async-start(bf16[64,2,512]{2,1,0:T(2,128)(2,1)} %reshape.558), calls=%async_computation | async-start | bytes 262144 | tf_op jit(solution)/shard_map/all_to_all | solution.py:53
  35.6 9.4 %all-to-all-done = bf16[64,2,512]{2,1,0:T(2,128)(2,1)S(1)} async-done(((bf16[64,2,512]{2,1,0:T(2,128)(2,1)}), bf16[64,2,512]{2,1,0:T(2,128)(2,1)S(1)}, u32[]{:S(2)}, u32[]{:S(2)}) %all-to-all-start) | async-done | bytes 131104 | tf_op jit(solution)/shard_map/all_to_all | solution.py:53
  45.0 4.9 all-to-all-start.5
  50.9 9.4 %all-to-all-done.5 = bf16[64,2,512]{2,1,0:T(2,128)(2,1)S(1)} async-done(((bf16[64,2,512]{2,1,0:T(2,128)(2,1)}), bf16[64,2,512]{2,1,0:T(2,128)(2,1)S(1)}, u32[]{:S(2)}, u32[]{:S(2)}) %all-to-all-start.5) | async-done | bytes 131104 | tf_op jit(solution)/shard_map/all_to_all | solution.py:53
  60.3 4.9 all-to-all-start.1
  68.8 8.4 %all-to-all-done.1 = f32[64,2,512]{2,1,0:T(2,128)S(1)} async-done(((f32[64,2,512]{2,1,0:T(2,128)}), f32[64,2,512]{2,1,0:T(2,128)S(1)}, u32[]{:S(2)}, u32[]{:S(2)}) %all-to-all-start.1) | async-done | bytes 262176 | tf_op jit(solution)/shard_map/all_to_all | solution.py:140
  77.2 6.4 %all-to-all-start.6 = ((f32[2,1,64,2,2,512]{5,3,4,0,1,2:T(2,128)}), f32[2,1,64,2,2,512]{5,3,4,0,1,2:T(2,128)S(1)}, u32[]{:S(2)}, u32[]{:S(2)}) async-start(f32[2,1,64,2,2,512]{5,3,4,0,1,2:T(2,128)} %copy.108), calls=%async_computation.6 | async-start | bytes 2097152 | tf_op jit(solution)/shard_map/all_to_all | solution.py:79
  96.5 15.6 %all-to-all-done.6 = f32[2,1,64,2,2,512]{5,3,4,0,1,2:T(2,128)S(1)} async-done(((f32[2,1,64,2,2,512]{5,3,4,0,1,2:T(2,128)}), f32[2,1,64,2,2,512]{5,3,4,0,1,2:T(2,128)S(1)}, u32[]{:S(2)}, u32[]{:S(2)}) %all-to-all-start.6) | async-done | bytes 1048608 | tf_op jit(solution)/shard_map/all_to_all | solution.py:79
  113.0 6.8 %all-to-all-start.2 = ((f32[2,2,64,2,2,512]{5,3,4,1,0,2:T(2,128)}), f32[2,2,64,2,2,512]{5,3,4,1,0,2:T(2,128)S(1)}, u32[]{:S(2)}, u32[]{:S(2)}) async-start(f32[2,2,64,2,2,512]{5,3,4,1,0,2:T(2,128)} %copy.100), calls=%async_computation.2 | async-start | bytes 4194304 | tf_op jit(solution)/shard_map/all_to_all | solution.py:79
  129.4 41.6 %all-to-all-done.2 = f32[2,2,64,2,2,512]{5,3,4,1,0,2:T(2,128)S(1)} async-done(((f32[2,2,64,2,2,512]{5,3,4,1,0,2:T(2,128)}), f32[2,2,64,2,2,512]{5,3,4,1,0,2:T(2,128)S(1)}, u32[]{:S(2)}, u32[]{:S(2)}) %all-to-all-start.2) | async-done | bytes 2097184 | tf_op jit(solution)/shard_map/all_to_all | solution.py:79
  187.9 6.3 %all-to-all-start.3 = ((f32[2,1,2,64,2,512]{5,4,2,1,0,3:T(2,128)}), f32[2,1,2,64,2,512]{5,4,2,1,0,3:T(2,128)}, u32[]{:S(2)}, u32[]{:S(2)}) async-start(f32[2,1,2,64,2,512]{5,4,2,1,0,3:T(2,128)} %copy.105), calls=%async_computation.3 | async-start | bytes 2097152 | tf_op jit(solution)/shard_map/all_to_all | solution.py:106
  206.3 16.1 %all-to-all-done.3 = f32[2,1,2,64,2,512]{5,4,2,1,0,3:T(2,128)} async-done(((f32[2,1,2,64,2,512]{5,4,2,1,0,3:T(2,128)}), f32[2,1,2,64,2,512]{5,4,2,1,0,3:T(2,128)}, u32[]{:S(2)}, u32[]{:S(2)}) %all-to-all-start.3) | async-done | bytes 1048608 | tf_op jit(solution)/shard_map/all_to_all | solution.py:106
  222.5 6.2 %all-to-all-start.7 = ((f32[2,2,2,64,2,512]{5,4,2,1,0,3:T(2,128)}), f32[2,2,2,64,2,512]{5,4,2,1,0,3:T(2,128)S(1)}, u32[]{:S(2)}, u32[]{:S(2)}) async-start(f32[2,2,2,64,2,512]{5,4,2,1,0,3:T(2,128)} %copy.112), calls=%async_computation.7 | async-start | bytes 4194304 | tf_op jit(solution)/shard_map/all_to_all | solution.py:106
  237.4 42.5 %all-to-all-done.7 = f32[2,2,2,64,2,512]{5,4,2,1,0,3:T(2,128)S(1)} async-done(((f32[2,2,2,64,2,512]{5,4,2,1,0,3:T(2,128)}), f32[2,2,2,64,2,512]{5,4,2,1,0,3:T(2,128)S(1)}, u32[]{:S(2)}, u32[]{:S(2)}) %all-to-all-start.7) | async-done | bytes 2097184 | tf_op jit(solution)/shard_map/all_to_all | solution.py:106
  279.9 6.1 %all-to-all-start.4 = ((f32[1,64,2,512]{3,2,0,1:T(2,128)}), f32[1,64,2,512]{3,2,0,1:T(2,128)S(1)}, u32[]{:S(2)}, u32[]{:S(2)}) async-start(f32[1,64,2,512]{3,2,0,1:T(2,128)} %copy.69), calls=%async_computation.4 | async-start | bytes 524288 | tf_op jit(solution)/shard_map/all_to_all | solution.py:112
  293.9 4.0 all-to-all-done.4
  297.9 6.3 %all-to-all-start.8 = ((f32[2,64,2,512]{3,2,0,1:T(2,128)}), f32[2,64,2,512]{3,2,0,1:T(2,128)S(1)}, u32[]{:S(2)}, u32[]{:S(2)}) async-start(f32[2,64,2,512]{3,2,0,1:T(2,128)} %copy.83), calls=%async_computation.8 | async-start | bytes 1048576 | tf_op jit(solution)/shard_map/all_to_all | solution.py:112
  304.4 17.1 %all-to-all-done.8 = f32[2,64,2,512]{3,2,0,1:T(2,128)S(1)} async-done(((f32[2,64,2,512]{3,2,0,1:T(2,128)}), f32[2,64,2,512]{3,2,0,1:T(2,128)S(1)}, u32[]{:S(2)}, u32[]{:S(2)}) %all-to-all-start.8) | async-done | bytes 524320 | tf_op jit(solution)/shard_map/all_to_all | solution.py:112
  324.7 242.6 %all-reduce = (f32[3,512]{1,0:T(4,128)S(1)}, f32[512]{0:T(512)S(1)}, f32[]{:T(128)}) all-reduce(f32[3,512]{1,0:T(4,128)S(1)} %pad_maximum_fusion.23, f32[512]{0:T(512)S(1)} %get-tuple-element.13, f32[]{:T(128)} %get-tuple-element.34), channel_id=1, replica_groups=mesh['ctx'=64,'ch'=8] {'ctx'}, use_global_device_ids=true, to_apply=%region_3.4 | all-reduce | flops 2049 | bytes 16392 | tf_op jit(solution)/shard_map/psum | solution.py:198
  574.4 8.4 %collective-permute-start.3 = (f32[2,512]{1,0:T(2,128)S(1)}, f32[2,512]{1,0:T(2,128)S(1)}, u32[]{:S(2)}, u32[]{:S(2)}) collective-permute-start(f32[2,512]{1,0:T(2,128)S(1)} %slice.213), channel_id=1, source_target_pairs={{8,0},{16,8},{24,16},{32,24},{40,32},{48,40},{56,48},{64,56},{72,6... | collective-permute-start | bytes 12296 | tf_op jit(solution)/shard_map/ppermute | solution.py:13
  587.3 4.9 collective-permute-start.7
  593.2 7.3 %collective-permute-start.8 = (f32[]{:T(128)}, f32[]{:T(128)}, u32[]{:S(2)}, u32[]{:S(2)}) collective-permute-start(f32[]{:T(128)} %add.297), channel_id=1, source_target_pairs={{0,4},{1,5},{2,6},{3,7},{4,0},{5,1},{6,2},{7,3},{8,12},{9,13},{10,... | collective-permute-start | bytes 20 | tf_op jit(solution)/shard_map/ppermute | solution.py:202
  (118 shorter events, 101.4 us)
Async XLA Ops:
  1.3 15.8 %collective-permute-start.2 = (bf16[2,512]{1,0:T(2,128)(2,1)S(1)}, bf16[2,512]{1,0:T(2,128)(2,1)S(1)}, u32[]{:S(2)}, u32[]{:S(2)}) collective-permute-start(bf16[2,512]{1,0:T(2,128)(2,1)S(1)} %slice.167), channel_id=1, source_target_pairs={{0,8},{8,16},{16,24},{24,32},{32,40},{40,48},{48,56},{56,64},{64,7... | collective-permute-start | bytes 6152 | tf_op jit(solution)/shard_map/ppermute | solution.py:13
  7.4 8.8 %collective-permute-start.1 = (bf16[2,512]{1,0:T(2,128)(2,1)S(1)}, bf16[2,512]{1,0:T(2,128)(2,1)S(1)}, u32[]{:S(2)}, u32[]{:S(2)}) collective-permute-start(bf16[2,512]{1,0:T(2,128)(2,1)S(1)} %slice.163), channel_id=1, source_target_pairs={{0,8},{8,16},{16,24},{24,32},{32,40},{40,48},{48,56},{56,64},{64,7... | collective-permute-start | bytes 6152 | tf_op jit(solution)/shard_map/ppermute | solution.py:13
  10.1 5.2 collective-permute-start
  18.1 16.7 %copy-start.9 = (bf16[128,512]{1,0:T(8,128)(2,1)S(1)}, bf16[128,512]{1,0:T(8,128)(2,1)}, u32[]{:S(2)}) copy-start(bf16[128,512]{1,0:T(8,128)(2,1)} %param.10) | copy-start | bytes 393220
  18.1 31.8 %copy-start.11 = (f32[128,512]{1,0:T(8,128)S(1)}, f32[128,512]{1,0:T(8,128)}, u32[]{:S(2)}) copy-start(f32[128,512]{1,0:T(8,128)} %param.12) | copy-start | bytes 786436
  20.2 45.6 %copy-start.7 = (bf16[128,512]{1,0:T(8,128)(2,1)}, bf16[128,512]{1,0:T(8,128)(2,1)S(1)}, u32[]{:S(2)}) copy-start(bf16[128,512]{1,0:T(8,128)(2,1)S(1)} %get-tuple-element.14) | copy-start | bytes 393220
  20.9 24.2 %all-to-all-start = ((bf16[64,2,512]{2,1,0:T(2,128)(2,1)}), bf16[64,2,512]{2,1,0:T(2,128)(2,1)S(1)}, u32[]{:S(2)}, u32[]{:S(2)}) async-start(bf16[64,2,512]{2,1,0:T(2,128)(2,1)} %reshape.558), calls=%async_computation | async-start | bytes 262144 | tf_op jit(solution)/shard_map/all_to_all | solution.py:53
  45.0 15.2 %all-to-all-start.5 = ((bf16[64,2,512]{2,1,0:T(2,128)(2,1)}), bf16[64,2,512]{2,1,0:T(2,128)(2,1)S(1)}, u32[]{:S(2)}, u32[]{:S(2)}) async-start(bf16[64,2,512]{2,1,0:T(2,128)(2,1)} %reshape.563), calls=%async_computation.5 | async-start | bytes 262144 | tf_op jit(solution)/shard_map/all_to_all | solution.py:53
  60.3 16.9 %all-to-all-start.1 = ((f32[64,2,512]{2,1,0:T(2,128)}), f32[64,2,512]{2,1,0:T(2,128)S(1)}, u32[]{:S(2)}, u32[]{:S(2)}) async-start(f32[64,2,512]{2,1,0:T(2,128)} %reshape.559), calls=%async_computation.1 | async-start | bytes 524288 | tf_op jit(solution)/shard_map/all_to_all | solution.py:140
  77.2 34.9 %all-to-all-start.6 = ((f32[2,1,64,2,2,512]{5,3,4,0,1,2:T(2,128)}), f32[2,1,64,2,2,512]{5,3,4,0,1,2:T(2,128)S(1)}, u32[]{:S(2)}, u32[]{:S(2)}) async-start(f32[2,1,64,2,2,512]{5,3,4,0,1,2:T(2,128)} %copy.108), calls=%async_computation.6 | async-start | bytes 2097152 | tf_op jit(solution)/shard_map/all_to_all | solution.py:79
  113.0 58.0 %all-to-all-start.2 = ((f32[2,2,64,2,2,512]{5,3,4,1,0,2:T(2,128)}), f32[2,2,64,2,2,512]{5,3,4,1,0,2:T(2,128)S(1)}, u32[]{:S(2)}, u32[]{:S(2)}) async-start(f32[2,2,64,2,2,512]{5,3,4,1,0,2:T(2,128)} %copy.100), calls=%async_computation.2 | async-start | bytes 4194304 | tf_op jit(solution)/shard_map/all_to_all | solution.py:79
  187.9 34.6 %all-to-all-start.3 = ((f32[2,1,2,64,2,512]{5,4,2,1,0,3:T(2,128)}), f32[2,1,2,64,2,512]{5,4,2,1,0,3:T(2,128)}, u32[]{:S(2)}, u32[]{:S(2)}) async-start(f32[2,1,2,64,2,512]{5,4,2,1,0,3:T(2,128)} %copy.105), calls=%async_computation.3 | async-start | bytes 2097152 | tf_op jit(solution)/shard_map/all_to_all | solution.py:106
  222.5 57.4 %all-to-all-start.7 = ((f32[2,2,2,64,2,512]{5,4,2,1,0,3:T(2,128)}), f32[2,2,2,64,2,512]{5,4,2,1,0,3:T(2,128)S(1)}, u32[]{:S(2)}, u32[]{:S(2)}) async-start(f32[2,2,2,64,2,512]{5,4,2,1,0,3:T(2,128)} %copy.112), calls=%async_computation.7 | async-start | bytes 4194304 | tf_op jit(solution)/shard_map/all_to_all | solution.py:106
  279.9 18.0 %all-to-all-start.4 = ((f32[1,64,2,512]{3,2,0,1:T(2,128)}), f32[1,64,2,512]{3,2,0,1:T(2,128)S(1)}, u32[]{:S(2)}, u32[]{:S(2)}) async-start(f32[1,64,2,512]{3,2,0,1:T(2,128)} %copy.69), calls=%async_computation.4 | async-start | bytes 524288 | tf_op jit(solution)/shard_map/all_to_all | solution.py:112
  292.7 30.0 %copy-start.8 = (bf16[128,512]{1,0:T(8,128)(2,1)S(1)}, bf16[128,512]{1,0:T(8,128)(2,1)}, u32[]{:S(2)}) copy-start(bf16[128,512]{1,0:T(8,128)(2,1)} %copy-done.7) | copy-start | bytes 393220
  292.7 30.0 %copy-start.10 = (bf16[128,512]{1,0:T(8,128)(2,1)S(1)}, bf16[128,512]{1,0:T(8,128)(2,1)}, u32[]{:S(2)}) copy-start(bf16[128,512]{1,0:T(8,128)(2,1)} %param.10) | copy-start | bytes 393220
  292.7 30.0 %copy-start.12 = (f32[512]{0:T(512)S(1)}, f32[512]{0:T(512)}, u32[]{:S(2)}) copy-start(f32[512]{0:T(512)} %param.13) | copy-start | bytes 6148
  297.9 23.6 %all-to-all-start.8 = ((f32[2,64,2,512]{3,2,0,1:T(2,128)}), f32[2,64,2,512]{3,2,0,1:T(2,128)S(1)}, u32[]{:S(2)}, u32[]{:S(2)}) async-start(f32[2,64,2,512]{3,2,0,1:T(2,128)} %copy.83), calls=%async_computation.8 | async-start | bytes 1048576 | tf_op jit(solution)/shard_map/all_to_all | solution.py:112
  570.5 16.2 %collective-permute-start.6 = (f32[]{:T(128)}, f32[]{:T(128)}, u32[]{:S(2)}, u32[]{:S(2)}) collective-permute-start(f32[]{:T(128)} %add.295), channel_id=1, source_target_pairs={{0,1},{1,0},{2,3},{3,2},{4,5},{5,4},{6,7},{7,6},{8,9},{9,8},{10,11... | collective-permute-start | bytes 20 | tf_op jit(solution)/shard_map/ppermute | solution.py:202
  574.4 30.0 %collective-permute-start.3 = (f32[2,512]{1,0:T(2,128)S(1)}, f32[2,512]{1,0:T(2,128)S(1)}, u32[]{:S(2)}, u32[]{:S(2)}) collective-permute-start(f32[2,512]{1,0:T(2,128)S(1)} %slice.213), channel_id=1, source_target_pairs={{8,0},{16,8},{24,16},{32,24},{40,32},{48,40},{56,48},{64,56},{72,6... | collective-permute-start | bytes 12296 | tf_op jit(solution)/shard_map/ppermute | solution.py:13
  582.8 21.6 %collective-permute-start.4 = (f32[2,512]{1,0:T(2,128)S(1)}, f32[2,512]{1,0:T(2,128)S(1)}, u32[]{:S(2)}, u32[]{:S(2)}) collective-permute-start(f32[2,512]{1,0:T(2,128)S(1)} %slice.223), channel_id=1, source_target_pairs={{8,0},{16,8},{24,16},{32,24},{40,32},{48,40},{56,48},{64,56},{72,6... | collective-permute-start | bytes 12296 | tf_op jit(solution)/shard_map/ppermute | solution.py:13
  584.7 19.7 %collective-permute-start.5 = (f32[2,512]{1,0:T(2,128)S(1)}, f32[2,512]{1,0:T(2,128)S(1)}, u32[]{:S(2)}, u32[]{:S(2)}) collective-permute-start(f32[2,512]{1,0:T(2,128)S(1)} %slice.226), channel_id=1, source_target_pairs={{8,0},{16,8},{24,16},{32,24},{40,32},{48,40},{56,48},{64,56},{72,6... | collective-permute-start | bytes 12296 | tf_op jit(solution)/shard_map/ppermute | solution.py:13
  587.3 5.3 collective-permute-start.7
  593.2 8.3 %collective-permute-start.8 = (f32[]{:T(128)}, f32[]{:T(128)}, u32[]{:S(2)}, u32[]{:S(2)}) collective-permute-start(f32[]{:T(128)} %add.297), channel_id=1, source_target_pairs={{0,4},{1,5},{2,6},{3,7},{4,0},{5,1},{6,2},{7,3},{8,12},{9,13},{10,... | collective-permute-start | bytes 20 | tf_op jit(solution)/shard_map/ppermute | solution.py:202
  (7 other events, 8.9 us)
